TPU v7x, 512 devices: a whole 4x4x16 slice. The times are simulated.
512 devices in a mesh: train: 32 (over x, z_lo), query: 16 (over z_hi, y, core).
Axes of the slice: x: 4, y: 4, z: 16 (z_hi: 2, z_lo: 8; z = z_hi * 8 + z_lo), core: 2. Of those that a mesh axis runs over, the one named last changes fastest.
Arguments:
- train_factors: bfloat16 [32768, 16, 128], P(('train', 'query'))
- query_factors: bfloat16 [8192, 16, 128], P(('query', 'train'))
Outputs:
- scores: float32 [32768, 8192], P('train', 'query')
All inputs are finite; a program needn't handle non-finite values.
Results may differ from a plain program's by a relative error of at most 0.0041.
Values may be sent and summed in bfloat16 or wider, within the bound.
A program may use at most 128 MiB of HBM per device.

v0:
```python
import jax
import jax.numpy as jnp
from jax import lax
from jax.sharding import PartitionSpec as P


def sequence_grads(factors):
    width = factors.shape[2] // 2
    length = factors.shape[1]
    first = factors[:, :, :width]
    second = factors[:, :, width:]
    grads = jnp.einsum("sti,stj->sij", first, second, preferred_element_type=jnp.float32) / length
    return grads


def inverse_of(cov, width):
    damped = cov + 0.1 * (jnp.trace(cov) / width) * jnp.eye(width, dtype=jnp.float32)
    lower = jnp.linalg.cholesky(damped)
    return jax.scipy.linalg.cho_solve((lower, True), jnp.eye(width, dtype=jnp.float32))


def precondition_factors(factors, inv_in, inv_out):
    count = factors.shape[0]
    length = factors.shape[1]
    width = factors.shape[2] // 2
    first = factors[:, :, :width].reshape(count * length, width).astype(jnp.float32)
    second = factors[:, :, width:].reshape(count * length, width).astype(jnp.float32)
    left = jnp.dot(first, inv_in, precision=lax.Precision.HIGHEST).reshape(count, length, width)
    right = jnp.dot(second, inv_out, precision=lax.Precision.HIGHEST).reshape(count, length, width)
    return jnp.einsum("sti,stj->sij", left, right, precision=lax.Precision.HIGHEST) / length


def score_tile(train_rows, query_rows):
    product = lax.dot_general(
        train_rows, query_rows, (((1,), (1,)), ((), ())), preferred_element_type=jnp.float32
    )
    return product * 0.125


def body(train_factors, query_factors):
    width = train_factors.shape[2] // 2
    length = train_factors.shape[1]
    first = train_factors[:, :, :width]
    second = train_factors[:, :, width:]
    part_in = lax.dot_general(
        first, first, (((0, 1), (0, 1)), ((), ())), preferred_element_type=jnp.float32
    )
    part_out = lax.dot_general(
        second, second, (((0, 1), (0, 1)), ((), ())), preferred_element_type=jnp.float32
    )
    total_in, total_out = lax.psum((part_in, part_out), ("train", "query"))
    count = train_factors.shape[0] * length * lax.axis_size("train") * lax.axis_size("query")
    inv_in = inverse_of(total_in / count, width)
    inv_out = inverse_of(total_out / count, width)
    pre = precondition_factors(query_factors, inv_in, inv_out)
    query_pre = pre.reshape(query_factors.shape[0], width * width).astype(jnp.bfloat16)
    query_all = lax.all_gather(query_pre, "train", axis=0, tiled=True)
    train_grads = (
        sequence_grads(train_factors)
        .reshape(train_factors.shape[0], width * width)
        .astype(jnp.bfloat16)
    )
    return score_tile(lax.all_gather(train_grads, "query", axis=0, tiled=True), query_all)


def solution(mesh):
    return jax.shard_map(
        body,
        mesh=mesh,
        in_specs=(P(("train", "query"), None, None), P(("query", "train"), None, None)),
        out_specs=P("train", "query"),
        check_vma=False,
    )
```

profile of v0, /device:TPU:1, one launch (start us, length us, event | category | flops | bytes accessed | tf_op | source)
XLA Modules:
  0.0 581.2 jit_solution(8863233645786744561)
XLA Ops:
  6.5 1.0 fusion.20
  7.5 1.2 fusion.19
  8.7 0.2 convolution_bitcast_fusion.2
  9.0 0.2 convolution_bitcast_fusion.3
  9.2 111.3 %all-reduce = (f32[64,64]{0,1:T(8,128)S(1)}, f32[64,64]{0,1:T(8,128)S(1)}) all-reduce(f32[64,64]{0,1:T(8,128)S(1)} %convolution_bitcast_fusion.3, f32[64,64]{0,1:T(8,128)S(1)} %convolution_bitcast_fusion.2), channel_id=1, replica_groups=mesh['train'=32,'query'=16] {'train','query'}, use_global_device_ids=true, to_apply=%region_0.0 | all-reduce | flops 8192 | bytes 65536 | tf_op jit(solution)/shard_map/psum | solution.py:51
  120.5 0.6 select_reduce_fusion.2
  121.1 0.7 select_reduce_fusion.3
  123.2 0.1 copy.21
  123.3 5.8 %cholesky.55 = f32[64,64]{1,0:T(8,128)S(1)} custom-call(f32[64,64]{1,0:T(8,128)S(1)} %fusion.12), custom_call_target="Cholesky" | custom-call | tf_op jit(solution)/shard_map/jit(cholesky)/cholesky | solution.py:18
  129.2 0.6 compare_reduce_fusion
  129.8 0.7 fusion.8
  130.5 4.9 custom-call.9
  135.4 0.3 fusion.3
  135.6 0.2 fusion.9
  135.9 5.8 %cholesky.44 = f32[64,64]{1,0:T(8,128)S(1)} custom-call(f32[64,64]{1,0:T(8,128)S(1)} %fusion.16), custom_call_target="Cholesky" | custom-call | tf_op jit(solution)/shard_map/jit(cholesky)/cholesky | solution.py:18
  141.8 0.6 compare_reduce_fusion.1
  142.4 0.7 fusion.7
  143.1 4.9 custom-call.8
  148.0 0.3 fusion.5
  148.2 0.2 fusion.13
  148.4 0.2 convolution_bitcast_fusion.1
  148.6 0.1 copy.17
  148.7 0.2 convolution_bitcast_fusion
  149.0 0.1 copy.22
  149.1 1.0 fusion
  150.1 0.9 convert_element_type.26
  151.1 0.2 all-gather.3.cloned.1.call-start
  151.3 0.6 multiply_convert_fusion
  151.9 1.6 convert_element_type.23
  153.5 208.7 %all-gather.5.cloned.1.call-done = bf16[512,4096]{1,0:T(8,128)(2,1)} async-done(((bf16[16,4096]{1,0:T(8,128)(2,1)}), bf16[512,4096]{1,0:T(8,128)(2,1)}) %all-gather.5.cloned.1.call-update) | async-done | bytes 4194320 | tf_op jit(solution)/shard_map/all_gather | solution.py:57
  362.2 201.8 %all-gather.3.cloned.1.call-done = bf16[1024,4096]{1,0:T(8,128)(2,1)} async-done(((bf16[64,4096]{1,0:T(8,128)(2,1)}), bf16[1024,4096]{1,0:T(8,128)(2,1)}) %all-gather.3.cloned.1.call-update) | async-done | bytes 8388624 | tf_op jit(solution)/shard_map/all_gather | solution.py:63
  564.0 10.4 %convolution_multiply_fusion = f32[1024,512]{1,0:T(8,128)} fusion(bf16[1024,4096]{1,0:T(8,128)(2,1)} %all-gather.3.cloned.1.call-done, bf16[512,4096]{1,0:T(8,128)(2,1)} %all-gather.5.cloned.1.call-done), kind=kOutput, calls=%fused_computation.1 | convolution fusion | flops 4295491584 | bytes 14680064 | tf_op jit(solution)/shard_map/dot_general | solution.py:34
  (11 shorter events, 0.2 us)
Async XLA Ops:
  6.5 144.8 %copy-start = (bf16[64,16,128]{2,1,0:T(8,128)(2,1)S(1)}, bf16[64,16,128]{2,1,0:T(8,128)(2,1)}, u32[]{:S(2)}) copy-start(bf16[64,16,128]{2,1,0:T(8,128)(2,1)} %param.5) | copy-start | bytes 786436
  6.5 355.7 %all-gather.5.cloned.1.call-start = ((), (), s32[]{:S(2)}) async-start(), calls=%async_computation.1 | async-start | bytes 4325376 | tf_op jit(solution)/shard_map/all_gather | solution.py:57
  151.1 412.9 %all-gather.3.cloned.1.call-start = ((), (), s32[]{:S(2)}) async-start(), calls=%async_computation | async-start | bytes 8912896 | tf_op jit(solution)/shard_map/all_gather | solution.py:63
Sparse Core Ops, SparseCore 0:
  151.2 210.9 all-gather.4
  365.5 198.3 all-gather.2
where the time goes:
time: 582 us; the launch traced here: 581 us
  waiting for transfers between devices  410 us (70%)
  blocking collectives  111 us (19%)
  other arithmetic  25.5 us (4%)
  between operations  14.9 us (3%)
  matrix products  13.8 us (2%)
    all_gather x1, waiting for transfers between devices, body(): query_all = lax.all_gather(query_pre, 'train', axis=0, tiled=True)  209 us
    all_gather x1, waiting for transfers between devices, body(): lax.all_gather(train_grads, 'query', axis=0, tiled=True)  202 us
    psum x1, blocking collectives, body(): total_in, total_out = lax.psum((part_in, part_out), ('train', 'query'))  111 us
    another operation x6, other arithmetic, inverse_of(): lower = jnp.linalg.cholesky(damped)  13 us
  transfers between devices with their start and end apart: 2, of which 2 were waited for; matrix products, arithmetic and copies ran while one was open for 0% of the time, Pallas kernels for 0%

commit v1 on v0

v1 whole, which is shorter than its diff:
```python
import functools

import jax
import jax.numpy as jnp
from jax import lax
from jax.experimental import pallas as pl
from jax.experimental.pallas import tpu as pltpu
from jax.sharding import PartitionSpec as P

MESH = pl.DeviceIdType.MESH
F32 = jnp.float32
BF16 = jnp.bfloat16

NX, NY, NZ, ZLO = 4, 4, 16, 8
UNIT = 256
NEWTON = 8


def coordinates():
    t = lax.axis_index("train")
    q = lax.axis_index("query")
    return t // ZLO, (q // 2) % NY, (q // (2 * NY)) * ZLO + t % ZLO, q % 2


def device(x, y, z, c):
    return (x * ZLO + z % ZLO, (z // ZLO) * (2 * NY) + y * 2 + c)


def iota(shape, dim):
    return lax.broadcasted_iota(jnp.int32, shape, dim)


def split2(v):
    hi = v.astype(BF16)
    return hi, (v - hi.astype(F32)).astype(BF16)


def mm(a, b):
    return jnp.dot(a, b, preferred_element_type=F32)


def mm3(a, b):
    ah, al = split2(a)
    bh, bl = split2(b)
    return mm(ah, bh) + (mm(ah, bl) + mm(al, bh))


def mmh(a, b):
    return jnp.dot(a, b, preferred_element_type=F32, precision=lax.Precision.HIGHEST)


def inverse_pair(total, tokens):
    row, lane = iota((64, 128), 0), iota((64, 128), 1)
    cov = total * (1.0 / tokens)
    first = lane < 64
    tr_in = jnp.sum(jnp.where(lane == row, cov, 0.0)) * (1.0 / 64)
    tr_out = jnp.sum(jnp.where(lane == row + 64, cov, 0.0)) * (1.0 / 64)
    top = jnp.where(first, cov + jnp.where(lane == row, 0.1 * tr_in, 0.0), 0.0)
    bottom = jnp.where(first, 0.0, cov + jnp.where(lane == row + 64, 0.1 * tr_out, 0.0))
    damped = jnp.concatenate([top, bottom], axis=0)
    r, l = iota((128, 128), 0), iota((128, 128), 1)
    eye = jnp.where(r == l, 1.0, 0.0)
    low, high = 0.1, 64.1
    seed = 2.0 / (low + high)
    inv = jnp.where(r == l, jnp.where(r < 64, seed / tr_in, seed / tr_out), 0.0)
    bound = 2.0 * low / (low + high)
    for step in range(NEWTON):
        mul = mmh if step >= NEWTON - 2 else mm3
        mapped = bound * (2.0 - bound)
        scale = 2.0 / (1.0 + mapped) if step < NEWTON - 2 else 1.0
        inv = scale * mul(inv, 2.0 * eye - mul(damped, inv))
        bound = 2.0 * mapped / (1.0 + mapped)
    return inv


def expand(first_t, mask):
    base = jnp.concatenate([first_t[:32], first_t[32:]], axis=1)
    rows = [jnp.broadcast_to(base[i : i + 1], (8, 256)) * mask for i in range(32)]
    return jnp.concatenate(rows, axis=0).astype(BF16)


def spread(second, rolled, group):
    left = iota((128, 128), 1) < 64
    if group == 0:
        return jnp.concatenate([jnp.where(left, second, 0.0), jnp.where(left, 0.0, rolled)], axis=0)
    return jnp.concatenate([jnp.where(left, rolled, 0.0), jnp.where(left, 0.0, second)], axis=0)


def store_rows(out_ref, row, pair, scale):
    a, b = pair
    for i in range(32):
        tile = jnp.concatenate([a[8 * i : 8 * i + 8], b[8 * i : 8 * i + 8]], axis=0) * scale
        out_ref[pl.ds(row, 16), 128 * i : 128 * i + 128] = tile.astype(BF16)


def kernel(
    tokens, train_ref, query_ref, out_ref, tbuf, qbuf, grads, pre, part, sibpart, half, rs, zs, ag, total,
    sib_s, sib_r, small_s, small_r, tz_s, tz_r, ty_s, ty_r, tzy_s, tzy_r, tc_s, tc_r, qq_s, qq_r, qx_s, qx_r,
):
    x, y, z, c = coordinates()
    me_t = lax.axis_index("train")
    me_q = lax.axis_index("query")
    plane = x * NY + y
    sibling = device(x, y, z, 1 - c)
    plane_peers = [
        (lax.rem(x + dx, NX), lax.rem(y + dy, NY)) for dx in range(NX) for dy in range(NY) if dx or dy
    ]
    z_peers = [lax.rem(z + dz, NZ) for dz in range(1, NZ)]

    barrier = pltpu.get_barrier_semaphore()
    for pz in z_peers:
        pl.semaphore_signal(barrier, inc=1, device_id=device(x, y, pz, c), device_id_type=MESH)
    for px, py in plane_peers:
        pl.semaphore_signal(barrier, inc=1, device_id=device(px, py, z, c), device_id_type=MESH)
    pl.semaphore_signal(barrier, inc=1, device_id=sibling, device_id_type=MESH)

    left = iota((128, 128), 1) < 64

    def arrange(src, at, dst, block, to):
        a = src[pl.ds(at, 128), :]
        b = src[pl.ds(at + 128, 128), :]
        a32, b32 = a.astype(F32), b.astype(F32)
        at32, bt32 = a32.T, b32.T
        dst[block, pl.ds(to, 64), :] = at32[:64].astype(BF16)
        dst[block, pl.ds(to + 64, 64), :] = bt32[:64].astype(BF16)
        dst[block, pl.ds(to + 128, 128), :] = jnp.where(left, pltpu.roll(a32, 64, 1), b32).astype(BF16)
        return a, b, at32.astype(BF16), bt32.astype(BF16)

    cov = jnp.zeros((128, 128), F32)
    for u in range(4):
        a, b, at, bt = arrange(train_ref, u * UNIT, tbuf, me_q, u * UNIT)
        cov = cov + mm(at, a) + mm(bt, b)
    arrange(query_ref, 0, qbuf, me_t, 0)
    part[...] = jnp.where(iota((64, 128), 1) < 64, cov[:64], cov[64:])

    pl.semaphore_wait(barrier, 31)

    sends = []

    def send(src, dst, ssem, rsem, to):
        cp = pltpu.make_async_remote_copy(
            src_ref=src, dst_ref=dst, send_sem=ssem, recv_sem=rsem, device_id=to, device_id_type=MESH
        )
        cp.start()
        sends.append(cp)
        return cp

    def arrived(dst, ssem, rsem):
        pltpu.make_async_remote_copy(
            src_ref=dst, dst_ref=dst, send_sem=ssem, recv_sem=rsem, device_id=sibling, device_id_type=MESH
        ).wait_recv()

    pair = send(part, sibpart, sib_s, sib_r, sibling)
    far = lax.rem(z + 8, NZ)
    far_q = lax.rem(me_q + 8, 16)

    def rows(block, h):
        return tbuf.at[block, pl.ds(512 * h, 512)]

    def far_send(h):
        return send(rows(me_q, h), rows(me_q, h), tz_s.at[h], tz_r.at[h], device(x, y, far, c))

    first_far = far_send(0)
    zlo = lax.rem(z, ZLO)
    zbase = z - zlo
    quad = zlo - lax.rem(zlo, 4)

    def quad_peer(d):
        return quad + lax.rem(zlo + d, 4)

    def unit_send(block, sem, to):
        return send(qbuf.at[block], qbuf.at[block], qq_s.at[sem], qq_r.at[sem], device(x, y, zbase + to, c))

    partner = lax.rem(zlo + 4, ZLO)
    unit_send(me_t, 3, partner)
    for d in (1, 2, 3):
        unit_send(me_t, d - 1, quad_peer(d))
    for dy in (1, 2, 3):
        send(tbuf.at[me_q], tbuf.at[me_q], ty_s.at[dy - 1], ty_r.at[dy - 1], device(x, lax.rem(y + dy, NY), z, c))
    send(tbuf.at[me_q], tbuf.at[me_q], tc_s.at[0], tc_r.at[0], sibling)

    pair.wait_recv()
    mine = part[...] + sibpart[...]
    for k in range(16):
        half[k] = mine[4 * k : 4 * k + 4]

    def small(stage, src_of, dst, slot, peers):
        for src, to in zip(src_of, peers, strict=True):
            pltpu.make_async_remote_copy(
                src_ref=src, dst_ref=dst.at[slot], send_sem=small_s.at[stage], recv_sem=small_r.at[stage],
                device_id=to, device_id_type=MESH,
            ).start()

    def small_wait(stage, buf, recv):
        w = pltpu.make_async_remote_copy(
            src_ref=buf.at[pl.ds(0, 15)], dst_ref=buf.at[pl.ds(0, 15)], send_sem=small_s.at[stage],
            recv_sem=small_r.at[stage], device_id=sibling, device_id_type=MESH,
        )
        if recv:
            w.wait_recv()
        else:
            w.wait_send()

    plane_to = [device(px, py, z, c) for px, py in plane_peers]
    small(0, [half.at[px * NY + py] for px, py in plane_peers], rs, plane, plane_to)
    rs[plane] = half[plane]

    mask = jnp.where(iota((8, 256), 1) // 16 % 8 == iota((8, 256), 0), 1.0, 0.0)

    def form_unit(block, u):
        at = pl.multiple_of(u * UNIT, UNIT)
        second = tbuf[block, pl.ds(at + 128, 128), :].astype(F32)
        rolled = pltpu.roll(second, 64, 1)
        outs = []
        for g in range(2):
            lhs = expand(tbuf[block, pl.ds(at + 64 * g, 64), :].astype(F32), mask)
            outs.append(mm(lhs, spread(second, rolled, g).astype(BF16)))
        row = pl.multiple_of(block * 64 + u * 16, 16)
        store_rows(grads, row, outs, 1.0 / 16)

    def form(blocks, lo, hi):
        for block in blocks:

            @pl.loop(lo, hi)
            def _(u, block=block):
                form_unit(block, u)

    own = [me_q - 2 * y + 2 * lax.rem(y + dy, NY) for dy in range(NY)]
    from_y = [me_q - 2 * y + 2 * lax.rem(y + NY - dy, NY) for dy in range(NY)]
    far_from_y = [lax.rem(b + 8, 16) for b in from_y]

    def other(block):
        return block + 1 - 2 * c

    form([me_q], 0, 4)

    small_wait(0, rs, True)
    piece = rs[0]
    for k in range(1, 16):
        piece = piece + rs[k]
    zs[z] = piece
    small(1, [zs.at[z]] * 15, zs, z, [device(x, y, pz, c) for pz in z_peers])

    arrived(qbuf.at[me_t], qq_s.at[3], qq_r.at[3])
    partner_t = me_t - zlo + partner
    for d in (1, 2, 3):
        unit_send(partner_t, 3 + d, quad_peer(d))
    arrived(tbuf.at[me_q], tc_s.at[0], tc_r.at[0])
    form([other(me_q)], 0, 4)
    for dy in (1, 2, 3):
        arrived(tbuf.at[me_q], ty_s.at[dy - 1], ty_r.at[dy - 1])
        send(tbuf.at[from_y[dy]], tbuf.at[from_y[dy]], tc_s.at[dy], tc_r.at[dy], sibling)
    form([from_y[1]], 0, 4)

    small_wait(1, zs, True)
    piece = zs[0]
    for k in range(1, 16):
        piece = piece + zs[k]
    ag[plane] = piece
    small(2, [ag.at[plane]] * 15, ag, plane, plane_to)

    first_far.wait_send()
    far_send(1)
    for d in (1, 2, 3):
        arrived(qbuf.at[me_t], qq_s.at[d - 1], qq_r.at[d - 1])

    def x_send(s, at):
        src = qbuf.at[pl.ds(x * ZLO + at, 4)]
        for dx in (1, 2, 3):
            send(src, src, qx_s.at[3 * s + dx - 1], qx_r.at[3 * s + dx - 1], device(lax.rem(x + dx, NX), y, z, c))

    x_send(0, quad)
    form([from_y[2]], 0, 4)

    small_wait(2, ag, True)
    for k in range(16):
        total[4 * k : 4 * k + 4] = ag[k]
    inv = inverse_pair(total[...], tokens)

    def far_recv(h):
        arrived(rows(me_q, h), tz_s.at[h], tz_r.at[h])
        for dy in (1, 2, 3):
            i = 3 * h + dy - 1
            send(
                rows(far_q, h), rows(far_q, h), tzy_s.at[i], tzy_r.at[i], device(x, lax.rem(y + dy, NY), z, c)
            )
        send(rows(far_q, h), rows(far_q, h), tc_s.at[4 + h], tc_r.at[4 + h], sibling)

    far_recv(0)
    for d in (1, 2, 3):
        arrived(qbuf.at[me_t], qq_s.at[3 + d], qq_r.at[3 + d])
    x_send(1, 4 - quad)
    form([from_y[3]], 0, 4)
    for dy in (1, 2, 3):
        arrived(tbuf.at[me_q], tc_s.at[dy], tc_r.at[dy])
    form([other(b) for b in from_y[1:]], 0, 4)

    in_parts, out_parts = [], []
    lane64 = iota((64, 128), 1) < 64
    top, bottom = inv[:64], inv[64:]
    w_in = jnp.concatenate([top, pltpu.roll(top, 64, 1)], axis=0)
    w_out = jnp.concatenate([pltpu.roll(bottom, 64, 1), bottom], axis=0)
    in_h, in_l = split2(w_in)
    out_h, out_l = split2(w_out)

    for s in range(2):
        for dx in (1, 2, 3):
            arrived(qbuf.at[pl.ds(0, 4)], qx_s.at[3 * s + dx - 1], qx_r.at[3 * s + dx - 1])

    @pl.loop(0, 32)
    def _(b):
        first = qbuf[b, pl.ds(0, 128), :]
        second = qbuf[b, pl.ds(128, 128), :]
        first_p = mm(in_h, first) + mm(in_l, first)
        second_p = mm(second, out_h) + mm(second, out_l)
        rolled = pltpu.roll(second_p, 64, 1)
        outs = []
        for g in range(2):
            part_t = first_p[64 * g : 64 * g + 64]
            hi = part_t.astype(BF16).astype(F32)
            lhs_h = expand(hi, mask)
            lhs_l = expand(part_t - hi, mask)
            rhs = spread(second_p, rolled, g)
            rhs_h, rhs_l = split2(rhs)
            outs.append(mm(lhs_h, rhs_h) + (mm(lhs_h, rhs_l) + mm(lhs_l, rhs_h)))
        store_rows(pre, pl.multiple_of(b * 16, 16), outs, 1.0 / 16)

    far_recv(1)

    def product(zhi):
        for m in range(2):
            for n in range(2):
                at = pl.multiple_of(zhi * 512 + m * 256, 256)
                tile = lax.dot_general(
                    grads[pl.ds(at, 256), :], pre[256 * n : 256 * n + 256, :], (((1,), (1,)), ((), ())),
                    preferred_element_type=F32,
                )
                out_ref[pl.ds(at, 256), 256 * n : 256 * n + 256] = tile * 0.125

    zhi = z // ZLO
    product(zhi)

    for h in range(2):
        for dy in (1, 2, 3):
            i = 3 * h + dy - 1
            arrived(rows(me_q, h), tzy_s.at[i], tzy_r.at[i])
            b = far_from_y[dy]
            send(rows(b, h), rows(b, h), tc_s.at[6 + i], tc_r.at[6 + i], sibling)
        form(far_from_y, 2 * h, 2 * h + 2)
        arrived(rows(me_q, h), tc_s.at[4 + h], tc_r.at[4 + h])
        for dy in (1, 2, 3):
            i = 3 * h + dy - 1
            arrived(rows(me_q, h), tc_s.at[6 + i], tc_r.at[6 + i])
        form([other(b) for b in far_from_y], 2 * h, 2 * h + 2)
    product(1 - zhi)

    for cp in sends:
        if cp is not first_far:
            cp.wait_send()
    small_wait(0, rs, False)
    small_wait(1, zs, False)
    small_wait(2, ag, False)


def body(train_factors, query_factors):
    tokens = train_factors.shape[0] * train_factors.shape[1] * 512
    train = train_factors.reshape(-1, 128)
    query = query_factors.reshape(-1, 128)
    vmem = pl.BlockSpec(memory_space=pltpu.VMEM)
    dma = pltpu.SemaphoreType.DMA
    return pl.pallas_call(
        functools.partial(kernel, tokens),
        out_shape=jax.ShapeDtypeStruct((1024, 512), F32),
        in_specs=[vmem, vmem],
        out_specs=vmem,
        scratch_shapes=[
            pltpu.VMEM((16, 1024, 128), BF16),
            pltpu.VMEM((32, 256, 128), BF16),
            pltpu.VMEM((1024, 4096), BF16),
            pltpu.VMEM((512, 4096), BF16),
            pltpu.VMEM((64, 128), F32),
            pltpu.VMEM((64, 128), F32),
            pltpu.VMEM((16, 4, 128), F32),
            pltpu.VMEM((16, 4, 128), F32),
            pltpu.VMEM((16, 4, 128), F32),
            pltpu.VMEM((16, 4, 128), F32),
            pltpu.VMEM((64, 128), F32),
            dma, dma, dma((3,)), dma((3,)), dma((2,)), dma((2,)), dma((3,)), dma((3,)), dma((6,)), dma((6,)),
            dma((12,)), dma((12,)), dma((7,)), dma((7,)), dma((6,)), dma((6,)),
        ],
        compiler_params=pltpu.CompilerParams(
            collective_id=0, has_side_effects=True, vmem_limit_bytes=48 * 2**20
        ),
        name="influence",
    )(train, query)


def solution(mesh):
    return jax.shard_map(
        body,
        mesh=mesh,
        in_specs=(P(("train", "query"), None, None), P(("query", "train"), None, None)),
        out_specs=P("train", "query"),
        check_vma=False,
    )
```

time: 582 us -> 106 us (0.18)
  waiting for transfers between devices: 410 us -> 0 us
  blocking collectives: 111 us -> 0 us
  Pallas kernels: 0 us -> 103 us
  other arithmetic: 25.5 us -> 0 us
  between operations: 14.9 us -> 0.01 us
  matrix products: 13.8 us -> 0 us
    all_gather x2 -> x0, waiting for transfers between devices: 410 us -> none  [the longest x1 209 us: body(): query_all = lax.all_gather(query_pre, 'train', axis=0, tiled=True)]
    psum x1 -> x0, blocking collectives: 111 us -> none  [body(): total_in, total_out = lax.psum((part_in, part_out), ('train', 'query'))]
    pallas_call x0 -> x1, Pallas kernels: none -> 103 us  [body(): pl.pallas_call(functools.partial(kernel, tokens), out_shape=jax.ShapeDtyp...]
    another operation x10 -> x0, other arithmetic: 24.1 us -> none  [the longest x6 13 us: inverse_of(): lower = jnp.linalg.cholesky(damped)]
    dot_general x7 -> x0, matrix products: 13 us -> none  [the longest x1 10.4 us: score_tile(): lax.dot_general(train_rows, query_rows, (((1,), (1,)), ((), ())), preferr...]
  transfers between devices with their start and end apart: 2 -> 0, of which waited for: 2 -> 0; matrix products, arithmetic and copies ran while one was open for 0% -> 0% of each run, Pallas kernels for 0% -> 0%
where the time goes in v1:
time: 106 us
  Pallas kernels  103 us (97%)
  local copies, waits for them, and re-layouts  3.11 us (3%)
    pallas_call x1, Pallas kernels, body(): pl.pallas_call(functools.partial(kernel, tokens), out_shape=jax.ShapeDtyp...  103 us
    unnamed x5, local copies, waits for them, and re-layouts  3.11 us

profile of v1, /device:TPU:1, one launch (start us, length us, event | category | flops | bytes accessed | tf_op | source)
XLA Modules:
  0.0 106.1 jit_solution(10094008604614218742)
XLA Ops:
  0.0 0.0 copy-start
  0.0 0.9 copy-done
  1.0 0.0 copy-start.1
  1.0 0.8 copy-done.1
  1.8 102.9 %influence.1 = f32[1024,512]{1,0:T(8,128)S(1)} custom-call(bf16[1024,128]{1,0:T(8,128)(2,1)S(1)} %bitcast.2, bf16[256,128]{1,0:T(8,128)(2,1)S(1)} %bitcast.3), custom_call_target="tpu_custom_call" | custom-call | tf_op jit(solution)/shard_map/influence/pallas_call | solution.py:371
  104.7 1.3 %copy.4 = f32[1024,512]{1,0:T(8,128)} copy(f32[1024,512]{1,0:T(8,128)S(1)} %influence.1) | data formatting | bytes 4194304
Async XLA Ops:
  0.0 0.9 copy-start
  1.0 0.8 copy-start.1

commit v2 on v0

v2 whole, which is shorter than its diff:
```python
import functools

import jax
import jax.numpy as jnp
from jax import lax
from jax.experimental import pallas as pl
from jax.experimental.pallas import tpu as pltpu
from jax.sharding import PartitionSpec as P

MESH = pl.DeviceIdType.MESH
F32 = jnp.float32
BF16 = jnp.bfloat16

NX, NY, NZ, ZLO = 4, 4, 16, 8
UNIT = 256
HALF = 512
STAGE = 32
CHUNKS = 2
NEWTON = 8
LOW, HIGH = 0.1, 64.1


def coordinates():
    t = lax.axis_index("train")
    q = lax.axis_index("query")
    return t // ZLO, (q // 2) % NY, (q // (2 * NY)) * ZLO + t % ZLO, q % 2


def device(x, y, z, c):
    return (x * ZLO + z % ZLO, (z // ZLO) * (2 * NY) + y * 2 + c)


def iota(shape, dim):
    return lax.broadcasted_iota(jnp.int32, shape, dim)


def split2(v):
    hi = v.astype(BF16)
    return hi, (v - hi.astype(F32)).astype(BF16)


def mm(a, b):
    return jnp.dot(a, b, preferred_element_type=F32)


def mm3(a, b):
    ah, al = split2(a)
    bh, bl = split2(b)
    return mm(ah, bh) + (mm(ah, bl) + mm(al, bh))


def mmh(a, b):
    return jnp.dot(a, b, preferred_element_type=F32, precision=lax.Precision.HIGHEST)


def eye128():
    return jnp.where(iota((128, 128), 0) == iota((128, 128), 1), 1.0, 0.0)


def damp(total, tokens):
    row, lane = iota((64, 128), 0), iota((64, 128), 1)
    cov = total * (1.0 / tokens)
    first = lane < 64
    tr_in = jnp.sum(jnp.where(lane == row, cov, 0.0)) * (1.0 / 64)
    tr_out = jnp.sum(jnp.where(lane == row + 64, cov, 0.0)) * (1.0 / 64)
    top = jnp.where(first, cov + jnp.where(lane == row, 0.1 * tr_in, 0.0), 0.0)
    bottom = jnp.where(first, 0.0, cov + jnp.where(lane == row + 64, 0.1 * tr_out, 0.0))
    r, lanes = iota((128, 128), 0), iota((128, 128), 1)
    mean = jnp.where(r < 64, tr_in, tr_out)
    guess = jnp.where(r == lanes, (2.0 / (LOW + HIGH)) / mean, 0.0)
    return jnp.concatenate([top, bottom], axis=0), guess


def newton(damped, inv, lo, hi):
    bound = 2.0 * LOW / (LOW + HIGH)
    for step in range(hi):
        mapped = bound * (2.0 - bound)
        plain = step >= NEWTON - 2
        if step >= lo:
            mul = mmh if plain else mm3
            inv = mul(inv, 2.0 * eye128() - mul(damped, inv))
            if not plain:
                inv = inv * (2.0 / (1.0 + mapped))
        bound = 2.0 * mapped / (1.0 + mapped)
    return inv


def expand(first_t, mask):
    rows = []
    for i in range(32):
        a = jnp.broadcast_to(first_t[i : i + 1], (8, 128)) * mask
        b = jnp.broadcast_to(first_t[32 + i : 33 + i], (8, 128)) * mask
        rows.append(jnp.concatenate([a, b], axis=1))
    return jnp.concatenate(rows, axis=0)


def spread(second, rolled, group):
    left = iota((128, 128), 1) < 64
    zero = jnp.zeros_like(second)
    if group == 0:
        return jnp.concatenate([jnp.where(left, second, zero), jnp.where(left, zero, rolled)], axis=0)
    return jnp.concatenate([jnp.where(left, rolled, zero), jnp.where(left, zero, second)], axis=0)


def store_rows(out_ref, row, pair):
    a, b = pair
    for i in range(32):
        tile = jnp.concatenate([a[8 * i : 8 * i + 8], b[8 * i : 8 * i + 8]], axis=0)
        out_ref[pl.ds(row, 16), 128 * i : 128 * i + 128] = tile.astype(BF16)


def kernel(
    tokens, train_hbm, query_hbm, out_ref, train_ref, query_ref, tbuf, qbuf, grads, pre, ppre, part, sibpart, half, rs, zs,
    ag, total, damped, inv, in_sem, sib_s, sib_r, small_s, small_r, ring_s, ring_r, ku_s, ku_r, kd_s, kd_r, x_s, x_r,
    y_s, y_r, fy_s, fy_r, c_s, c_r,
):
    x, y, z, c = coordinates()
    me_t = lax.axis_index("train")
    me_q = lax.axis_index("query")
    plane = x * NY + y
    sibling = device(x, y, z, 1 - c)
    zlo = lax.rem(z, ZLO)
    zhi = z // ZLO
    plane_peers = [
        (lax.rem(x + dx, NX), lax.rem(y + dy, NY)) for dx in range(NX) for dy in range(NY) if dx or dy
    ]
    plane_to = [device(px, py, z, c) for px, py in plane_peers]
    z_to = [device(x, y, lax.rem(z + dz, NZ), c) for dz in range(1, NZ)]
    x_to = [device(lax.rem(x + d, NX), y, z, c) for d in range(NX)]
    y_to = [device(x, lax.rem(y + d, NY), z, c) for d in range(NY)]

    inputs = [
        pltpu.make_async_copy(train_hbm, train_ref, in_sem.at[0]),
        pltpu.make_async_copy(query_hbm, query_ref, in_sem.at[1]),
    ]
    for cp in inputs:
        cp.start()
    barrier = pltpu.get_barrier_semaphore()
    for to in [*z_to, *plane_to, sibling]:
        pl.semaphore_signal(barrier, inc=1, device_id=to, device_id_type=MESH)
    for cp in inputs:
        cp.wait()

    left = iota((128, 128), 1) < 64

    def arrange(src, at, dst, block, to):
        a = src[pl.ds(at, 128), :]
        b = src[pl.ds(at + 128, 128), :]
        a32, b32 = a.astype(F32), b.astype(F32)
        at32, bt32 = a32.T, b32.T
        dst[block, pl.ds(to, 64), :] = at32[:64].astype(BF16)
        dst[block, pl.ds(to + 64, 64), :] = bt32[:64].astype(BF16)
        dst[block, pl.ds(to + 128, 128), :] = jnp.where(left, pltpu.roll(a32, 64, 1), b32).astype(BF16)
        return a, b, at32.astype(BF16), bt32.astype(BF16)

    cov = jnp.zeros((128, 128), F32)
    for u in range(4):
        a, b, at, bt = arrange(train_ref, u * UNIT, tbuf, 2 * me_q + u // 2, (u % 2) * UNIT)
        cov = cov + mm(at, a) + mm(bt, b)
    arrange(query_ref, 0, qbuf, me_t, 0)
    part[...] = jnp.where(iota((64, 128), 1) < 64, cov[:64], cov[64:])

    pl.semaphore_wait(barrier, 31)

    def copy(src, dst, ssem, rsem, to=sibling):
        return pltpu.make_async_remote_copy(
            src_ref=src, dst_ref=dst, send_sem=ssem, recv_sem=rsem, device_id=to, device_id_type=MESH
        )

    rows = HALF // CHUNKS

    def ring_index(d, step):
        return (step * 2 + d) * CHUNKS

    def ring_slot(d, step, k):
        landed = 2 * lax.rem(me_q + 8, 16) + d
        return tbuf.at[jnp.where(step < 7, STAGE + d * 7 + step, landed), pl.ds(rows * k, rows)]

    def ring_send(d, step, k, src):
        zr = lax.rem(z + (1 if d == 0 else NZ - 1), NZ)
        landed = 2 * ((1 - zr // ZLO) * 8 + 2 * y + c) + d
        dst = tbuf.at[jnp.where(step < 7, STAGE + d * 7 + step, landed), pl.ds(rows * k, rows)]
        i = ring_index(d, step) + k
        copy(src, dst, ring_s.at[i], ring_r.at[i], device(x, y, zr, c)).start()

    def ring_recv(d, step, k):
        i = ring_index(d, step) + k
        slot = ring_slot(d, step, k)
        copy(slot, slot, ring_s.at[i], ring_r.at[i]).wait_recv()
        return slot

    def chain_units(s):
        return me_t - jnp.minimum(s, zlo), me_t + jnp.minimum(s, ZLO - 1 - zlo)

    def chain_send(s):
        up, down = chain_units(s)

        @pl.when((zlo >= s) & (zlo < ZLO - 1))
        def _():
            to = device(x, y, jnp.minimum(z + 1, NZ - 1), c)
            copy(qbuf.at[up], qbuf.at[up], ku_s.at[s], ku_r.at[s], to).start()

        @pl.when((zlo + s <= ZLO - 1) & (zlo > 0))
        def _():
            to = device(x, y, jnp.maximum(z - 1, 0), c)
            copy(qbuf.at[down], qbuf.at[down], kd_s.at[s], kd_r.at[s], to).start()

    def chain_recv(s):
        up, down = chain_units(s)

        @pl.when(zlo >= s)
        def _():
            copy(qbuf.at[up], qbuf.at[up], ku_s.at[s - 1], ku_r.at[s - 1]).wait_recv()

        @pl.when(zlo + s <= ZLO - 1)
        def _():
            copy(qbuf.at[down], qbuf.at[down], kd_s.at[s - 1], kd_r.at[s - 1]).wait_recv()

    def x_send(unit):
        for d in (1, 2, 3):
            copy(qbuf.at[unit], qbuf.at[unit], x_s.at[d - 1], x_r.at[d - 1], x_to[d]).start()

    def block(b):
        return tbuf.at[pl.ds(2 * b, 2)]

    def near(e):
        other = e // 4
        return me_q - lax.rem(me_q, 8) + 2 * lax.rem(y + NY - lax.rem(e, 4), NY) + (c + other - 2 * c * other)

    def far(e):
        return lax.rem(near(e) + 8, 16)

    copy(part, sibpart, sib_s, sib_r).start()
    for k in range(CHUNKS):
        for d in range(2):
            ring_send(d, 0, k, tbuf.at[2 * me_q + d, pl.ds(rows * k, rows)])
    chain_send(0)
    for d in (1, 2, 3):
        copy(block(me_q), block(me_q), y_s.at[d - 1], y_r.at[d - 1], y_to[d]).start()
    copy(block(me_q), block(me_q), c_s.at[0], c_r.at[0]).start()
    x_send(me_t)

    copy(part, sibpart, sib_s, sib_r).wait()
    mine = part[...] + sibpart[...]
    for k in range(16):
        half[k] = mine[4 * k : 4 * k + 4]

    def small(stage, sources, dst, slot, peers):
        for src, to in zip(sources, peers, strict=True):
            copy(src, dst.at[slot], small_s.at[stage], small_r.at[stage], to).start()

    def small_copy(stage, buf):
        return copy(buf.at[pl.ds(0, 15)], buf.at[pl.ds(0, 15)], small_s.at[stage], small_r.at[stage])

    def sum16(buf):
        piece = buf[0]
        for k in range(1, 16):
            piece = piece + buf[k]
        return piece

    small(0, [half.at[px * NY + py] for px, py in plane_peers], rs, plane, plane_to)
    rs[plane] = half[plane]

    mask = jnp.where(iota((8, 128), 1) // 16 == iota((8, 128), 0), 1.0 / 16, 0.0)

    def form(b):
        for u in range(4):
            hb, at = 2 * b + u // 2, (u % 2) * UNIT
            second = tbuf[hb, at + 128 : at + 256, :]
            rolled = pltpu.roll(second.astype(F32), 64, 1).astype(BF16)
            outs = []
            for g in range(2):
                lhs = expand(tbuf[hb, at + 64 * g : at + 64 * g + 64, :].astype(F32), mask).astype(BF16)
                outs.append(mm(lhs, spread(second, rolled, g)))
            store_rows(grads, pl.multiple_of(b * 64 + u * 16, 16), outs)

    @pl.loop(1, 8)
    def _(s):
        chain_recv(s)
        chain_send(s)
        for k in range(CHUNKS):
            for d in range(2):
                ring_send(d, s, k, ring_recv(d, s - 1, k))
        up, down = chain_units(s)
        pl.when(zlo >= s)(lambda: x_send(up))
        pl.when(zlo + s <= ZLO - 1)(lambda: x_send(down))

        @pl.when(s == 1)
        def _():
            small_copy(0, rs).wait_recv()
            zs[z] = sum16(rs)
            small(1, [zs.at[z]] * 15, zs, z, z_to)

        @pl.when(s == 4)
        def _():
            small_copy(1, zs).wait_recv()
            ag[plane] = sum16(zs)
            small(2, [ag.at[plane]] * 15, ag, plane, plane_to)

        e = s - 1

        @pl.when((e >= 1) & (e <= 3))
        def _():
            copy(block(near(e)), block(near(e)), y_s.at[e - 1], y_r.at[e - 1]).wait_recv()
            copy(block(near(e)), block(near(e)), c_s.at[e], c_r.at[e]).start()

        @pl.when(e >= 4)
        def _():
            copy(block(near(e)), block(near(e)), c_s.at[e - 4], c_r.at[e - 4]).wait_recv()

        form(near(e))

        @pl.when(s == 6)
        def _():
            small_copy(2, ag).wait_recv()
            for k in range(16):
                total[4 * k : 4 * k + 4] = ag[k]
            mat, guess = damp(total[...], tokens)
            damped[...] = mat
            inv[...] = newton(mat, guess, 0, 3)

        @pl.when(s == 7)
        def _():
            inv[...] = newton(damped[...], inv[...], 3, 6)

    far_b = far(0)
    for k in range(CHUNKS):
        for d in range(2):
            ring_recv(d, 7, k)
    for d in (1, 2, 3):
        copy(block(far_b), block(far_b), fy_s.at[d - 1], fy_r.at[d - 1], y_to[d]).start()
    copy(block(far_b), block(far_b), c_s.at[4], c_r.at[4]).start()

    inverse = newton(damped[...], inv[...], 6, NEWTON)
    copy(block(near(7)), block(near(7)), c_s.at[3], c_r.at[3]).wait_recv()

    top, bottom = inverse[:64], inverse[64:]
    in_h, in_l = split2(jnp.concatenate([top, pltpu.roll(top, 64, 1)], axis=0))
    out_h, out_l = split2(jnp.concatenate([pltpu.roll(bottom, 64, 1), bottom], axis=0))

    for d in (1, 2, 3):
        src = qbuf.at[pl.ds(lax.rem(x + NX - d, NX) * ZLO, ZLO)]
        copy(src, src, x_s.at[d - 1], x_r.at[d - 1]).wait_recv()

    @pl.loop(0, 32, unroll=4)
    def _(b):
        first = qbuf[b, 0:128, :]
        second = qbuf[b, 128:256, :]
        ppre[b, 0:128, :] = mm(in_h, first) + mm(in_l, first)
        ppre[b, 128:256, :] = mm(second, out_h) + mm(second, out_l)

    def form_query(b):
        second = ppre[b, 128:256, :]
        rolled = pltpu.roll(second, 64, 1)
        outs = []
        for g in range(2):
            lhs = expand(ppre[b, 64 * g : 64 * g + 64, :], mask)
            lhs_h, lhs_l = split2(lhs)
            rhs_h, rhs_l = split2(spread(second, rolled, g))
            both = mm(lhs_h, jnp.concatenate([rhs_h, rhs_l], axis=1))
            outs.append(both[:, :128] + both[:, 128:] + mm(lhs_l, rhs_h))
        store_rows(pre, pl.multiple_of(b * 16, 16), outs)

    @pl.loop(0, 8)
    def _(i):
        for u in range(4):
            form_query(4 * i + u)
        e = i - 3

        @pl.when((e >= 1) & (e <= 3))
        def _():
            copy(block(far(e)), block(far(e)), fy_s.at[e - 1], fy_r.at[e - 1]).wait_recv()
            copy(block(far(e)), block(far(e)), c_s.at[4 + e], c_r.at[4 + e]).start()

    def product(h):
        @pl.loop(0, 4)
        def _(i):
            at = pl.multiple_of(h * 512 + (i // 2) * 256, 256)
            to = pl.multiple_of((i % 2) * 256, 256)
            tile = lax.dot_general(
                grads[pl.ds(at, 256), :], pre[pl.ds(to, 256), :], (((1,), (1,)), ((), ())),
                preferred_element_type=F32,
            )
            out_ref[pl.ds(at, 256), pl.ds(to, 256)] = tile * 0.125

    form(near(7))
    product(zhi)

    @pl.loop(0, 8)
    def _(e):
        @pl.when(e >= 4)
        def _():
            copy(block(far(e)), block(far(e)), c_s.at[e], c_r.at[e]).wait_recv()

        form(far(e))

    product(1 - zhi)

    for d in (1, 2, 3):
        units = qbuf.at[pl.ds(0, ZLO)]
        copy(units, units, x_s.at[d - 1], x_r.at[d - 1]).wait_send()
        copy(block(0), block(0), y_s.at[d - 1], y_r.at[d - 1]).wait_send()
        copy(block(0), block(0), fy_s.at[d - 1], fy_r.at[d - 1]).wait_send()
    for stage, buf in ((0, rs), (1, zs), (2, ag)):
        small_copy(stage, buf).wait_send()

    @pl.loop(0, 8)
    def _(s):
        copy(block(0), block(0), c_s.at[s], c_r.at[s]).wait_send()
        for d in range(2):
            for k in range(CHUNKS):
                i = ring_index(d, s) + k
                slot = tbuf.at[0, pl.ds(0, rows)]
                copy(slot, slot, ring_s.at[i], ring_r.at[i]).wait_send()

        @pl.when((zlo >= s) & (zlo < ZLO - 1))
        def _():
            copy(qbuf.at[0], qbuf.at[0], ku_s.at[s], ku_r.at[s]).wait_send()

        @pl.when((zlo + s <= ZLO - 1) & (zlo > 0))
        def _():
            copy(qbuf.at[0], qbuf.at[0], kd_s.at[s], kd_r.at[s]).wait_send()


def body(train_factors, query_factors):
    tokens = train_factors.shape[0] * train_factors.shape[1] * 512
    train = train_factors.reshape(-1, 128)
    query = query_factors.reshape(-1, 128)
    hbm = pl.BlockSpec(memory_space=pl.ANY)
    dma = pltpu.SemaphoreType.DMA
    return pl.pallas_call(
        functools.partial(kernel, tokens),
        out_shape=jax.ShapeDtypeStruct((1024, 512), F32),
        in_specs=[hbm, hbm],
        out_specs=pl.BlockSpec(memory_space=pltpu.VMEM),
        scratch_shapes=[
            pltpu.VMEM((1024, 128), BF16),
            pltpu.VMEM((256, 128), BF16),
            pltpu.VMEM((STAGE + 14, HALF, 128), BF16),
            pltpu.VMEM((32, UNIT, 128), BF16),
            pltpu.VMEM((1024, 4096), BF16),
            pltpu.VMEM((512, 4096), BF16),
            pltpu.VMEM((32, UNIT, 128), F32),
            pltpu.VMEM((64, 128), F32),
            pltpu.VMEM((64, 128), F32),
            pltpu.VMEM((16, 4, 128), F32),
            pltpu.VMEM((16, 4, 128), F32),
            pltpu.VMEM((16, 4, 128), F32),
            pltpu.VMEM((16, 4, 128), F32),
            pltpu.VMEM((64, 128), F32),
            pltpu.VMEM((128, 128), F32),
            pltpu.VMEM((128, 128), F32),
            dma((2,)), dma, dma, dma((3,)), dma((3,)), dma((16 * CHUNKS,)), dma((16 * CHUNKS,)),
            dma((8,)), dma((8,)), dma((8,)), dma((8,)), dma((3,)), dma((3,)), dma((3,)), dma((3,)), dma((3,)), dma((3,)),
            dma((8,)), dma((8,)),
        ],
        compiler_params=pltpu.CompilerParams(
            collective_id=0, has_side_effects=True, vmem_limit_bytes=48 * 2**20
        ),
        name="influence",
    )(train, query)


def solution(mesh):
    return jax.shard_map(
        body,
        mesh=mesh,
        in_specs=(P(("train", "query"), None, None), P(("query", "train"), None, None)),
        out_specs=P("train", "query"),
        check_vma=False,
    )
```

time: 582 us -> 85.5 us (0.15)
  the two profiles are of different devices: /device:TPU:1 before, /device:TPU:2 now
where the time goes in v2:
time: 85.5 us; the launch traced here: 85.3 us
  Pallas kernels  82.2 us (96%)
  local copies, waits for them, and re-layouts  3.11 us (4%)
    pallas_call x1, Pallas kernels, body(): pl.pallas_call(functools.partial(kernel, tokens), out_shape=jax.ShapeDtyp...  82.2 us
    unnamed x5, local copies, waits for them, and re-layouts  3.11 us

profile of v2, /device:TPU:2, one launch (start us, length us, event | category | flops | bytes accessed | tf_op | source)
XLA Modules:
  0.0 85.3 jit_solution(1828916652110668045)
XLA Ops:
  0.0 0.0 copy-start
  0.0 0.9 %copy-done = bf16[64,16,128]{2,1,0:T(8,128)(2,1)S(1)} copy-done((bf16[64,16,128]{2,1,0:T(8,128)(2,1)S(1)}, bf16[64,16,128]{2,1,0:T(8,128)(2,1)}, u32[]{:S(2)}) %copy-start) | copy-done | bytes 262168
  1.0 0.0 copy-start.1
  1.0 0.8 copy-done.1
  1.8 82.2 %influence.1 = f32[1024,512]{1,0:T(8,128)S(1)} custom-call(bf16[1024,128]{1,0:T(8,128)(2,1)S(1)} %bitcast.2, bf16[256,128]{1,0:T(8,128)(2,1)S(1)} %bitcast.3), custom_call_target="tpu_custom_call" | custom-call | tf_op jit(solution)/shard_map/influence/pallas_call | solution.py:431
  84.0 1.3 %copy.4 = f32[1024,512]{1,0:T(8,128)} copy(f32[1024,512]{1,0:T(8,128)S(1)} %influence.1) | data formatting | bytes 4194304
Async XLA Ops:
  0.0 0.9 %copy-start = (bf16[64,16,128]{2,1,0:T(8,128)(2,1)S(1)}, bf16[64,16,128]{2,1,0:T(8,128)(2,1)}, u32[]{:S(2)}) copy-start(bf16[64,16,128]{2,1,0:T(8,128)(2,1)} %param.2) | copy-start | bytes 786436
  1.0 0.8 copy-start.1

commit v3 on v2

--- a/solution.py
+++ b/solution.py
@@ -16,6 +16,7 @@
 HALF = 512
 STAGE = 32
 CHUNKS = 2
+STOPS = 8
 NEWTON = 8
 LOW, HIGH = 0.1, 64.1
 
@@ -110,9 +111,9 @@
 
 
 def kernel(
-    tokens, train_hbm, query_hbm, out_ref, train_ref, query_ref, tbuf, qbuf, grads, pre, ppre, part, sibpart, half, rs, zs,
-    ag, total, damped, inv, in_sem, sib_s, sib_r, small_s, small_r, ring_s, ring_r, ku_s, ku_r, kd_s, kd_r, x_s, x_r,
-    y_s, y_r, fy_s, fy_r, c_s, c_r,
+    tokens, train_hbm, query_hbm, out_ref, train_ref, query_ref, tbuf, qbuf, grads, pre, part, sibpart, half, rs, zs,
+    ag, total, weights, in_sem, sib_s, sib_r, small_s, small_r, ring_s, ring_r, ku_s, ku_r, kd_s, kd_r, x_s, x_r,
+    y_s, y_r, fy_s, fy_r, g_s, g_r,
 ):
     x, y, z, c = coordinates()
     me_t = lax.axis_index("train")
@@ -174,12 +175,12 @@
 
     def ring_slot(d, step, k):
         landed = 2 * lax.rem(me_q + 8, 16) + d
-        return tbuf.at[jnp.where(step < 7, STAGE + d * 7 + step, landed), pl.ds(rows * k, rows)]
+        return tbuf.at[jnp.where(step < STOPS - 1, STAGE + d * 7 + step, landed), pl.ds(rows * k, rows)]
 
     def ring_send(d, step, k, src):
         zr = lax.rem(z + (1 if d == 0 else NZ - 1), NZ)
         landed = 2 * ((1 - zr // ZLO) * 8 + 2 * y + c) + d
-        dst = tbuf.at[jnp.where(step < 7, STAGE + d * 7 + step, landed), pl.ds(rows * k, rows)]
+        dst = tbuf.at[jnp.where(step < STOPS - 1, STAGE + d * 7 + step, landed), pl.ds(rows * k, rows)]
         i = ring_index(d, step) + k
         copy(src, dst, ring_s.at[i], ring_r.at[i], device(x, y, zr, c)).start()
 
@@ -216,9 +217,9 @@
         def _():
             copy(qbuf.at[down], qbuf.at[down], kd_s.at[s - 1], kd_r.at[s - 1]).wait_recv()
 
-    def x_send(unit):
+    def x_send(unit, j):
         for d in (1, 2, 3):
-            copy(qbuf.at[unit], qbuf.at[unit], x_s.at[d - 1], x_r.at[d - 1], x_to[d]).start()
+            copy(qbuf.at[unit], qbuf.at[unit], x_s.at[d - 1], x_r.at[16 * (d - 1) + j], x_to[d]).start()
 
     def block(b):
         return tbuf.at[pl.ds(2 * b, 2)]
@@ -237,8 +238,7 @@
     chain_send(0)
     for d in (1, 2, 3):
         copy(block(me_q), block(me_q), y_s.at[d - 1], y_r.at[d - 1], y_to[d]).start()
-    copy(block(me_q), block(me_q), c_s.at[0], c_r.at[0]).start()
-    x_send(me_t)
+    x_send(me_t, 0)
 
     copy(part, sibpart, sib_s, sib_r).wait()
     mine = part[...] + sibpart[...]
@@ -263,29 +263,94 @@
 
     mask = jnp.where(iota((8, 128), 1) // 16 == iota((8, 128), 0), 1.0 / 16, 0.0)
 
-    def form(b):
-        for u in range(4):
-            hb, at = 2 * b + u // 2, (u % 2) * UNIT
-            second = tbuf[hb, at + 128 : at + 256, :]
+    def form_half(hb, row):
+        for u in range(2):
+            second = tbuf[hb, u * UNIT + 128 : u * UNIT + 256, :]
             rolled = pltpu.roll(second.astype(F32), 64, 1).astype(BF16)
             outs = []
             for g in range(2):
-                lhs = expand(tbuf[hb, at + 64 * g : at + 64 * g + 64, :].astype(F32), mask).astype(BF16)
+                first = tbuf[hb, u * UNIT + 64 * g : u * UNIT + 64 * g + 64, :]
+                lhs = expand(first.astype(F32), mask).astype(BF16)
                 outs.append(mm(lhs, spread(second, rolled, g)))
-            store_rows(grads, pl.multiple_of(b * 64 + u * 16, 16), outs)
-
-    @pl.loop(1, 8)
+            store_rows(grads, pl.multiple_of(row + u * 16, 16), outs)
+
+    def form(b, row):
+        form_half(2 * b, row)
+        form_half(2 * b + 1, row + 32)
+
+    def grad_copy(row, i):
+        rows_of = grads.at[pl.ds(pl.multiple_of(row, 64), 64)]
+        return copy(rows_of, rows_of, g_s.at[i], g_r.at[i])
+
+    far_rows = (1 - zhi) * 512
+    far_y = [y, lax.rem(y + 3, NY), lax.rem(y + 1, NY), lax.rem(y + 2, NY)]
+
+    def query_units(units):
+        firsts, seconds = [], []
+        for b in units:
+            first = qbuf[b, 0:128, :]
+            second = qbuf[b, 128:256, :]
+            firsts.append(mm(weights[0], first) + mm(weights[1], first))
+            seconds.append(mm(second, weights[2]) + mm(second, weights[3]))
+        for b, first_p, second_p in zip(units, firsts, seconds, strict=True):
+            rolled = pltpu.roll(second_p, 64, 1)
+            outs = []
+            for g in range(2):
+                lhs_h, lhs_l = split2(expand(first_p[64 * g : 64 * g + 64], mask))
+                rhs_h, rhs_l = split2(spread(second_p, rolled, g))
+                both = mm(lhs_h, jnp.concatenate([rhs_h, rhs_l], axis=1))
+                outs.append(both[:, :128] + both[:, 128:] + mm(lhs_l, rhs_h))
+            store_rows(pre, pl.multiple_of(b * 16, 16), outs)
+
+    def query_batch(j):
+        far_z = j // 2
+        above = j % 2 == 1
+        shift = jnp.where(above, far_z, -far_z)
+
+        @pl.when((above & (far_z > 0) & (zlo + far_z <= ZLO - 1)) | (jnp.logical_not(above) & (zlo >= far_z)))
+        def _():
+            units = [lax.rem(x + NX - d, NX) * ZLO + zlo + shift for d in range(NX)]
+            for d in (1, 2, 3):
+                b = qbuf.at[units[d]]
+                copy(b, b, x_s.at[d - 1], x_r.at[16 * (d - 1) + j]).wait_recv()
+            query_units(units)
+
+    def far_half(e, d):
+        return tbuf.at[2 * far(e) + d]
+
+    def fy(e, d, i, to=0):
+        return copy(far_half(e, d), far_half(e, d), fy_s.at[i], fy_r.at[i], y_to[to])
+
+    def land():
+        for d in range(2):
+            for k in range(CHUNKS):
+                ring_recv(d, STOPS - 1, k)
+            fy(0, d, d, 1 if d == 0 else 3).start()
+        fy(0, 1, 2, 1).start()
+        fy(0, 0, 3, 3).start()
+
+    def pass_on():
+        fy(1, 0, 0).wait_recv()
+        fy(1, 0, 4, 1).start()
+        fy(3, 1, 1).wait_recv()
+        fy(3, 1, 5, 3).start()
+
+    @pl.loop(1, 9)
     def _(s):
         chain_recv(s)
         chain_send(s)
-        for k in range(CHUNKS):
-            for d in range(2):
-                ring_send(d, s, k, ring_recv(d, s - 1, k))
+
+        @pl.when(s < STOPS)
+        def _():
+            for k in range(CHUNKS):
+                for d in range(2):
+                    ring_send(d, s, k, ring_recv(d, s - 1, k))
+
         up, down = chain_units(s)
-        pl.when(zlo >= s)(lambda: x_send(up))
-        pl.when(zlo + s <= ZLO - 1)(lambda: x_send(down))
-
-        @pl.when(s == 1)
+        pl.when(zlo >= s)(lambda: x_send(up, 2 * s))
+        pl.when(zlo + s <= ZLO - 1)(lambda: x_send(down, 2 * s + 1))
+
+        @pl.when(s == 2)
         def _():
             small_copy(0, rs).wait_recv()
             zs[z] = sum16(rs)
@@ -302,116 +367,96 @@
         @pl.when((e >= 1) & (e <= 3))
         def _():
             copy(block(near(e)), block(near(e)), y_s.at[e - 1], y_r.at[e - 1]).wait_recv()
-            copy(block(near(e)), block(near(e)), c_s.at[e], c_r.at[e]).start()
-
-        @pl.when(e >= 4)
-        def _():
-            copy(block(near(e)), block(near(e)), c_s.at[e - 4], c_r.at[e - 4]).wait_recv()
-
-        form(near(e))
-
-        @pl.when(s == 6)
+
+        @pl.when(e <= 3)
+        def _():
+            form(near(e), 64 * near(e))
+            grad_copy(64 * near(e), e).start()
+
+        @pl.when(s == 5)
         def _():
             small_copy(2, ag).wait_recv()
             for k in range(16):
                 total[4 * k : 4 * k + 4] = ag[k]
             mat, guess = damp(total[...], tokens)
-            damped[...] = mat
-            inv[...] = newton(mat, guess, 0, 3)
-
-        @pl.when(s == 7)
-        def _():
-            inv[...] = newton(damped[...], inv[...], 3, 6)
-
-    far_b = far(0)
-    for k in range(CHUNKS):
-        for d in range(2):
-            ring_recv(d, 7, k)
-    for d in (1, 2, 3):
-        copy(block(far_b), block(far_b), fy_s.at[d - 1], fy_r.at[d - 1], y_to[d]).start()
-    copy(block(far_b), block(far_b), c_s.at[4], c_r.at[4]).start()
-
-    inverse = newton(damped[...], inv[...], 6, NEWTON)
-    copy(block(near(7)), block(near(7)), c_s.at[3], c_r.at[3]).wait_recv()
-
-    top, bottom = inverse[:64], inverse[64:]
-    in_h, in_l = split2(jnp.concatenate([top, pltpu.roll(top, 64, 1)], axis=0))
-    out_h, out_l = split2(jnp.concatenate([pltpu.roll(bottom, 64, 1), bottom], axis=0))
-
-    for d in (1, 2, 3):
-        src = qbuf.at[pl.ds(lax.rem(x + NX - d, NX) * ZLO, ZLO)]
-        copy(src, src, x_s.at[d - 1], x_r.at[d - 1]).wait_recv()
-
-    @pl.loop(0, 32, unroll=4)
-    def _(b):
-        first = qbuf[b, 0:128, :]
-        second = qbuf[b, 128:256, :]
-        ppre[b, 0:128, :] = mm(in_h, first) + mm(in_l, first)
-        ppre[b, 128:256, :] = mm(second, out_h) + mm(second, out_l)
-
-    def form_query(b):
-        second = ppre[b, 128:256, :]
-        rolled = pltpu.roll(second, 64, 1)
-        outs = []
-        for g in range(2):
-            lhs = expand(ppre[b, 64 * g : 64 * g + 64, :], mask)
-            lhs_h, lhs_l = split2(lhs)
-            rhs_h, rhs_l = split2(spread(second, rolled, g))
-            both = mm(lhs_h, jnp.concatenate([rhs_h, rhs_l], axis=1))
-            outs.append(both[:, :128] + both[:, 128:] + mm(lhs_l, rhs_h))
-        store_rows(pre, pl.multiple_of(b * 16, 16), outs)
-
-    @pl.loop(0, 8)
+            inverse = newton(mat, guess, 0, NEWTON)
+            top, bottom = inverse[:64], inverse[64:]
+            weights[0], weights[1] = split2(jnp.concatenate([top, pltpu.roll(top, 64, 1)], axis=0))
+            weights[2], weights[3] = split2(jnp.concatenate([pltpu.roll(bottom, 64, 1), bottom], axis=0))
+
+        pl.when(s == STOPS)(land)
+
+        @pl.loop(jnp.where(s <= 6, 0, 4 * (s - 6)), jnp.where(s <= 5, 0, jnp.where(s == 8, 16, 4 * (s - 5))))
+        def _(j):
+            query_batch(j)
+
+        pl.when(s == STOPS)(pass_on)
+
+    for e in range(4):
+        grad_copy(0, e).wait_recv()
+
+    @pl.loop(0, 2)
     def _(i):
-        for u in range(4):
-            form_query(4 * i + u)
-        e = i - 3
-
-        @pl.when((e >= 1) & (e <= 3))
-        def _():
-            copy(block(far(e)), block(far(e)), fy_s.at[e - 1], fy_r.at[e - 1]).wait_recv()
-            copy(block(far(e)), block(far(e)), c_s.at[4 + e], c_r.at[4 + e]).start()
-
-    def product(h):
-        @pl.loop(0, 4)
-        def _(i):
-            at = pl.multiple_of(h * 512 + (i // 2) * 256, 256)
-            to = pl.multiple_of((i % 2) * 256, 256)
-            tile = lax.dot_general(
-                grads[pl.ds(at, 256), :], pre[pl.ds(to, 256), :], (((1,), (1,)), ((), ())),
-                preferred_element_type=F32,
-            )
-            out_ref[pl.ds(at, 256), pl.ds(to, 256)] = tile * 0.125
-
-    form(near(7))
-    product(zhi)
-
-    @pl.loop(0, 8)
-    def _(e):
-        @pl.when(e >= 4)
-        def _():
-            copy(block(far(e)), block(far(e)), c_s.at[e], c_r.at[e]).wait_recv()
-
-        form(far(e))
-
-    product(1 - zhi)
+        at = pl.multiple_of(zhi * 512, 512)
+        to = pl.multiple_of(i * 256, 256)
+        tile = lax.dot_general(
+            grads[pl.ds(at, 512), :], pre[pl.ds(to, 256), :], (((1,), (1,)), ((), ())), preferred_element_type=F32
+        )
+        out_ref[pl.ds(at, 512), pl.ds(to, 256)] = tile * 0.125
+
+    @pl.loop(0, 4)
+    def _(i):
+        e = jnp.where(i == 2, 3, jnp.where(i == 3, 2, i))
+
+        @pl.when(i == 1)
+        def _():
+            fy(1, 1, 2).wait_recv()
+
+        @pl.when(i == 2)
+        def _():
+            fy(3, 0, 3).wait_recv()
+
+        @pl.when(i == 3)
+        def _():
+            fy(2, 0, 4).wait_recv()
+            fy(2, 1, 5).wait_recv()
+
+        row = far_rows + 128 * i + 64 * c
+        form(far(e), row)
+        grad_copy(row, 4 + i).start()
+
+    @pl.loop(0, 2)
+    def _(i):
+        grad_copy(0, 4 + 2 * i).wait_recv()
+        grad_copy(0, 5 + 2 * i).wait_recv()
+        at = pl.multiple_of(far_rows + 256 * i, 256)
+        tile = lax.dot_general(
+            grads[pl.ds(at, 256), :], pre[...], (((1,), (1,)), ((), ())), preferred_element_type=F32
+        )
+        for k in range(2):
+            to = far_rows + 128 * jnp.where(i == 0, far_y[k], far_y[2 + k])
+            out_ref[pl.ds(pl.multiple_of(to, 128), 128), :] = tile[128 * k : 128 * k + 128] * 0.125
 
     for d in (1, 2, 3):
         units = qbuf.at[pl.ds(0, ZLO)]
         copy(units, units, x_s.at[d - 1], x_r.at[d - 1]).wait_send()
         copy(block(0), block(0), y_s.at[d - 1], y_r.at[d - 1]).wait_send()
-        copy(block(0), block(0), fy_s.at[d - 1], fy_r.at[d - 1]).wait_send()
+    for i in range(6):
+        fy(0, 0, i).wait_send()
     for stage, buf in ((0, rs), (1, zs), (2, ag)):
         small_copy(stage, buf).wait_send()
 
     @pl.loop(0, 8)
     def _(s):
-        copy(block(0), block(0), c_s.at[s], c_r.at[s]).wait_send()
-        for d in range(2):
-            for k in range(CHUNKS):
-                i = ring_index(d, s) + k
-                slot = tbuf.at[0, pl.ds(0, rows)]
-                copy(slot, slot, ring_s.at[i], ring_r.at[i]).wait_send()
+        grad_copy(0, s).wait_send()
+
+        @pl.when(s < STOPS)
+        def _():
+            for d in range(2):
+                for k in range(CHUNKS):
+                    i = ring_index(d, s) + k
+                    slot = tbuf.at[0, pl.ds(0, rows)]
+                    copy(slot, slot, ring_s.at[i], ring_r.at[i]).wait_send()
 
         @pl.when((zlo >= s) & (zlo < ZLO - 1))
         def _():
@@ -426,7 +471,7 @@
     tokens = train_factors.shape[0] * train_factors.shape[1] * 512
     train = train_factors.reshape(-1, 128)
     query = query_factors.reshape(-1, 128)
-    hbm = pl.BlockSpec(memory_space=pl.ANY)
+    hbm = pl.BlockSpec(memory_space=pltpu.HBM)
     dma = pltpu.SemaphoreType.DMA
     return pl.pallas_call(
         functools.partial(kernel, tokens),
@@ -440,7 +485,6 @@
             pltpu.VMEM((32, UNIT, 128), BF16),
             pltpu.VMEM((1024, 4096), BF16),
             pltpu.VMEM((512, 4096), BF16),
-            pltpu.VMEM((32, UNIT, 128), F32),
             pltpu.VMEM((64, 128), F32),
             pltpu.VMEM((64, 128), F32),
             pltpu.VMEM((16, 4, 128), F32),
@@ -448,14 +492,13 @@
             pltpu.VMEM((16, 4, 128), F32),
             pltpu.VMEM((16, 4, 128), F32),
             pltpu.VMEM((64, 128), F32),
-            pltpu.VMEM((128, 128), F32),
-            pltpu.VMEM((128, 128), F32),
+            pltpu.VMEM((4, 128, 128), BF16),
             dma((2,)), dma, dma, dma((3,)), dma((3,)), dma((16 * CHUNKS,)), dma((16 * CHUNKS,)),
-            dma((8,)), dma((8,)), dma((8,)), dma((8,)), dma((3,)), dma((3,)), dma((3,)), dma((3,)), dma((3,)), dma((3,)),
+            dma((9,)), dma((9,)), dma((9,)), dma((9,)), dma((3,)), dma((48,)), dma((3,)), dma((3,)), dma((6,)), dma((6,)),
             dma((8,)), dma((8,)),
         ],
         compiler_params=pltpu.CompilerParams(
-            collective_id=0, has_side_effects=True, vmem_limit_bytes=48 * 2**20
+            collective_id=0, has_side_effects=True, vmem_limit_bytes=63 * 2**20
         ),
         name="influence",
     )(train, query)

time: 85.5 us -> 78.5 us (0.918)
  the two profiles are of different devices: /device:TPU:2 before, /device:TPU:1 now
where the time goes in v3:
time: 78.5 us; the launch traced here: 78.3 us
  Pallas kernels  75.2 us (96%)
  local copies, waits for them, and re-layouts  3.08 us (4%)
    pallas_call x1, Pallas kernels, body(): pl.pallas_call(functools.partial(kernel, tokens), out_shape=jax.ShapeDtyp...  75.2 us
    unnamed x1, local copies, waits for them, and re-layouts  3.08 us

profile of v3, /device:TPU:1, one launch (start us, length us, event | category | flops | bytes accessed | tf_op | source)
XLA Modules:
  0.0 78.3 jit_solution(1188322890663324462)
XLA Ops:
  0.0 75.2 %influence.1 = f32[1024,512]{1,0:T(8,128)} custom-call(bf16[1024,128]{1,0:T(8,128)(2,1)} %bitcast.2, bf16[256,128]{1,0:T(8,128)(2,1)} %bitcast.3), custom_call_target="tpu_custom_call" | custom-call | tf_op jit(solution)/shard_map/influence/pallas_call | solution.py:476
  75.2 3.1 %copy.4 = f32[1024,512]{1,0:T(8,128)} copy(f32[1024,512]{1,0:T(8,128)} %influence.1) | data formatting | bytes 4194304

commit v4 on v3

--- a/solution.py
+++ b/solution.py
@@ -321,31 +321,37 @@
     def fy(e, d, i, to=0):
         return copy(far_half(e, d), far_half(e, d), fy_s.at[i], fy_r.at[i], y_to[to])
 
+    def fyc(e, d, k, i, to=0):
+        part_of = tbuf.at[2 * far(e) + d, pl.ds(rows * k, rows)]
+        j = 6 + 2 * i + k
+        return copy(part_of, part_of, fy_s.at[j], fy_r.at[j], y_to[to])
+
     def land():
-        for d in range(2):
-            for k in range(CHUNKS):
+        for k in range(CHUNKS):
+            for d in range(2):
                 ring_recv(d, STOPS - 1, k)
-            fy(0, d, d, 1 if d == 0 else 3).start()
+                fyc(0, d, k, d, 1 if d == 0 else 3).start()
         fy(0, 1, 2, 1).start()
         fy(0, 0, 3, 3).start()
 
     def pass_on():
-        fy(1, 0, 0).wait_recv()
-        fy(1, 0, 4, 1).start()
-        fy(3, 1, 1).wait_recv()
-        fy(3, 1, 5, 3).start()
+        for k in range(CHUNKS):
+            fyc(1, 0, k, 0).wait_recv()
+            fyc(1, 0, k, 2, 1).start()
+            fyc(3, 1, k, 1).wait_recv()
+            fyc(3, 1, k, 3, 3).start()
 
     @pl.loop(1, 9)
     def _(s):
-        chain_recv(s)
-        chain_send(s)
-
         @pl.when(s < STOPS)
         def _():
             for k in range(CHUNKS):
                 for d in range(2):
                     ring_send(d, s, k, ring_recv(d, s - 1, k))
 
+        chain_recv(s)
+        chain_send(s)
+
         up, down = chain_units(s)
         pl.when(zlo >= s)(lambda: x_send(up, 2 * s))
         pl.when(zlo + s <= ZLO - 1)(lambda: x_send(down, 2 * s + 1))
@@ -356,7 +362,7 @@
             zs[z] = sum16(rs)
             small(1, [zs.at[z]] * 15, zs, z, z_to)
 
-        @pl.when(s == 4)
+        @pl.when(s == 5)
         def _():
             small_copy(1, zs).wait_recv()
             ag[plane] = sum16(zs)
@@ -373,7 +379,7 @@
             form(near(e), 64 * near(e))
             grad_copy(64 * near(e), e).start()
 
-        @pl.when(s == 5)
+        @pl.when(s == 6)
         def _():
             small_copy(2, ag).wait_recv()
             for k in range(16):
@@ -386,7 +392,7 @@
 
         pl.when(s == STOPS)(land)
 
-        @pl.loop(jnp.where(s <= 6, 0, 4 * (s - 6)), jnp.where(s <= 5, 0, jnp.where(s == 8, 16, 4 * (s - 5))))
+        @pl.loop(jnp.where(s == 8, 8, 0), jnp.where(s <= 6, 0, 8 * (s - 6)))
         def _(j):
             query_batch(j)
 
@@ -418,8 +424,9 @@
 
         @pl.when(i == 3)
         def _():
-            fy(2, 0, 4).wait_recv()
-            fy(2, 1, 5).wait_recv()
+            for k in range(CHUNKS):
+                fyc(2, 0, k, 2).wait_recv()
+                fyc(2, 1, k, 3).wait_recv()
 
         row = far_rows + 128 * i + 64 * c
         form(far(e), row)
@@ -441,8 +448,11 @@
         units = qbuf.at[pl.ds(0, ZLO)]
         copy(units, units, x_s.at[d - 1], x_r.at[d - 1]).wait_send()
         copy(block(0), block(0), y_s.at[d - 1], y_r.at[d - 1]).wait_send()
-    for i in range(6):
+    for i in (2, 3):
         fy(0, 0, i).wait_send()
+    for i in range(4):
+        for k in range(CHUNKS):
+            fyc(0, 0, k, i).wait_send()
     for stage, buf in ((0, rs), (1, zs), (2, ag)):
         small_copy(stage, buf).wait_send()
 
@@ -469,8 +479,8 @@
 
 def body(train_factors, query_factors):
     tokens = train_factors.shape[0] * train_factors.shape[1] * 512
-    train = train_factors.reshape(-1, 128)
-    query = query_factors.reshape(-1, 128)
+    train = pltpu.with_memory_space_constraint(train_factors.reshape(-1, 128), pltpu.HBM)
+    query = pltpu.with_memory_space_constraint(query_factors.reshape(-1, 128), pltpu.HBM)
     hbm = pl.BlockSpec(memory_space=pltpu.HBM)
     dma = pltpu.SemaphoreType.DMA
     return pl.pallas_call(
@@ -494,11 +504,11 @@
             pltpu.VMEM((64, 128), F32),
             pltpu.VMEM((4, 128, 128), BF16),
             dma((2,)), dma, dma, dma((3,)), dma((3,)), dma((16 * CHUNKS,)), dma((16 * CHUNKS,)),
-            dma((9,)), dma((9,)), dma((9,)), dma((9,)), dma((3,)), dma((48,)), dma((3,)), dma((3,)), dma((6,)), dma((6,)),
+            dma((9,)), dma((9,)), dma((9,)), dma((9,)), dma((3,)), dma((48,)), dma((3,)), dma((3,)), dma((14,)), dma((14,)),
             dma((8,)), dma((8,)),
         ],
         compiler_params=pltpu.CompilerParams(
-            collective_id=0, has_side_effects=True, vmem_limit_bytes=63 * 2**20
+            collective_id=0, has_side_effects=True, vmem_limit_bytes=48 * 2**20
         ),
         name="influence",
     )(train, query)

time: 78.5 us -> 76.6 us (0.976)
  local copies, waits for them, and re-layouts: 3.08 us -> 1.32 us
    unnamed x1, local copies, waits for them, and re-layouts: 3.08 us -> 1.32 us
where the time goes in v4:
time: 76.6 us; the launch traced here: 76.5 us
  Pallas kernels  75.1 us (98%)
  local copies, waits for them, and re-layouts  1.32 us (2%)
    pallas_call x1, Pallas kernels, body(): pl.pallas_call(functools.partial(kernel, tokens), out_shape=jax.ShapeDtyp...  75.1 us

profile of v4, /device:TPU:1, one launch (start us, length us, event | category | flops | bytes accessed | tf_op | source)
XLA Modules:
  0.0 76.5 jit_solution(3216807316961543724)
XLA Ops:
  0.0 75.1 %influence.1 = f32[1024,512]{1,0:T(8,128)S(1)} custom-call(bf16[1024,128]{1,0:T(8,128)(2,1)} %bitcast.2, bf16[256,128]{1,0:T(8,128)(2,1)} %bitcast.3), custom_call_target="tpu_custom_call" | custom-call | tf_op jit(solution)/shard_map/influence/pallas_call | solution.py:486
  75.1 1.3 %copy.4 = f32[1024,512]{1,0:T(8,128)} copy(f32[1024,512]{1,0:T(8,128)S(1)} %influence.1) | data formatting | bytes 4194304

commit v5 on v4

--- a/solution.py
+++ b/solution.py
@@ -182,12 +182,12 @@
         landed = 2 * ((1 - zr // ZLO) * 8 + 2 * y + c) + d
         dst = tbuf.at[jnp.where(step < STOPS - 1, STAGE + d * 7 + step, landed), pl.ds(rows * k, rows)]
         i = ring_index(d, step) + k
-        copy(src, dst, ring_s.at[i], ring_r.at[i], device(x, y, zr, c)).start()
+        copy(src, dst, ring_s, ring_r.at[i], device(x, y, zr, c)).start()
 
     def ring_recv(d, step, k):
         i = ring_index(d, step) + k
         slot = ring_slot(d, step, k)
-        copy(slot, slot, ring_s.at[i], ring_r.at[i]).wait_recv()
+        copy(slot, slot, ring_s, ring_r.at[i]).wait_recv()
         return slot
 
     def chain_units(s):
@@ -410,6 +410,25 @@
         )
         out_ref[pl.ds(at, 512), pl.ds(to, 256)] = tile * 0.125
 
+    ring_all = tbuf.at[pl.ds(0, 2 * STOPS)]
+    copy(ring_all, ring_all, ring_s, ring_r.at[0]).wait_send()
+    for d in (1, 2, 3):
+        units = qbuf.at[pl.ds(0, ZLO)]
+        copy(units, units, x_s.at[d - 1], x_r.at[d - 1]).wait_send()
+        copy(block(0), block(0), y_s.at[d - 1], y_r.at[d - 1]).wait_send()
+    for stage, buf in ((0, rs), (1, zs), (2, ag)):
+        small_copy(stage, buf).wait_send()
+
+    @pl.loop(0, 8)
+    def _(s):
+        @pl.when((zlo >= s) & (zlo < ZLO - 1))
+        def _():
+            copy(qbuf.at[0], qbuf.at[0], ku_s.at[s], ku_r.at[s]).wait_send()
+
+        @pl.when((zlo + s <= ZLO - 1) & (zlo > 0))
+        def _():
+            copy(qbuf.at[0], qbuf.at[0], kd_s.at[s], kd_r.at[s]).wait_send()
+
     @pl.loop(0, 4)
     def _(i):
         e = jnp.where(i == 2, 3, jnp.where(i == 3, 2, i))
@@ -444,37 +463,13 @@
             to = far_rows + 128 * jnp.where(i == 0, far_y[k], far_y[2 + k])
             out_ref[pl.ds(pl.multiple_of(to, 128), 128), :] = tile[128 * k : 128 * k + 128] * 0.125
 
-    for d in (1, 2, 3):
-        units = qbuf.at[pl.ds(0, ZLO)]
-        copy(units, units, x_s.at[d - 1], x_r.at[d - 1]).wait_send()
-        copy(block(0), block(0), y_s.at[d - 1], y_r.at[d - 1]).wait_send()
     for i in (2, 3):
         fy(0, 0, i).wait_send()
     for i in range(4):
         for k in range(CHUNKS):
             fyc(0, 0, k, i).wait_send()
-    for stage, buf in ((0, rs), (1, zs), (2, ag)):
-        small_copy(stage, buf).wait_send()
-
-    @pl.loop(0, 8)
-    def _(s):
-        grad_copy(0, s).wait_send()
-
-        @pl.when(s < STOPS)
-        def _():
-            for d in range(2):
-                for k in range(CHUNKS):
-                    i = ring_index(d, s) + k
-                    slot = tbuf.at[0, pl.ds(0, rows)]
-                    copy(slot, slot, ring_s.at[i], ring_r.at[i]).wait_send()
-
-        @pl.when((zlo >= s) & (zlo < ZLO - 1))
-        def _():
-            copy(qbuf.at[0], qbuf.at[0], ku_s.at[s], ku_r.at[s]).wait_send()
-
-        @pl.when((zlo + s <= ZLO - 1) & (zlo > 0))
-        def _():
-            copy(qbuf.at[0], qbuf.at[0], kd_s.at[s], kd_r.at[s]).wait_send()
+    for i in range(8):
+        grad_copy(0, i).wait_send()
 
 
 def body(train_factors, query_factors):
@@ -503,7 +498,7 @@
             pltpu.VMEM((16, 4, 128), F32),
             pltpu.VMEM((64, 128), F32),
             pltpu.VMEM((4, 128, 128), BF16),
-            dma((2,)), dma, dma, dma((3,)), dma((3,)), dma((16 * CHUNKS,)), dma((16 * CHUNKS,)),
+            dma((2,)), dma, dma, dma((3,)), dma((3,)), dma, dma((16 * CHUNKS,)),
             dma((9,)), dma((9,)), dma((9,)), dma((9,)), dma((3,)), dma((48,)), dma((3,)), dma((3,)), dma((14,)), dma((14,)),
             dma((8,)), dma((8,)),
         ],

time: 76.6 us -> 76.3 us (level)
  no operation moved by 1% of the time
where the time goes in v5:
time: 76.3 us; the launch traced here: 76.2 us
  Pallas kernels  74.9 us (98%)
  local copies, waits for them, and re-layouts  1.32 us (2%)
    pallas_call x1, Pallas kernels, body(): pl.pallas_call(functools.partial(kernel, tokens), out_shape=jax.ShapeDtyp...  74.9 us

profile of v5, /device:TPU:1, one launch (start us, length us, event | category | flops | bytes accessed | tf_op | source)
XLA Modules:
  0.0 76.2 jit_solution(4375631851234130081)
XLA Ops:
  0.0 74.9 %influence.1 = f32[1024,512]{1,0:T(8,128)S(1)} custom-call(bf16[1024,128]{1,0:T(8,128)(2,1)} %bitcast.2, bf16[256,128]{1,0:T(8,128)(2,1)} %bitcast.3), custom_call_target="tpu_custom_call" | custom-call | tf_op jit(solution)/shard_map/influence/pallas_call | solution.py:481
  74.9 1.3 %copy.4 = f32[1024,512]{1,0:T(8,128)} copy(f32[1024,512]{1,0:T(8,128)S(1)} %influence.1) | data formatting | bytes 4194304

commit v6 on v5

--- a/solution.py
+++ b/solution.py
@@ -236,9 +236,6 @@
         for d in range(2):
             ring_send(d, 0, k, tbuf.at[2 * me_q + d, pl.ds(rows * k, rows)])
     chain_send(0)
-    for d in (1, 2, 3):
-        copy(block(me_q), block(me_q), y_s.at[d - 1], y_r.at[d - 1], y_to[d]).start()
-    x_send(me_t, 0)
 
     copy(part, sibpart, sib_s, sib_r).wait()
     mine = part[...] + sibpart[...]
@@ -260,6 +257,9 @@
 
     small(0, [half.at[px * NY + py] for px, py in plane_peers], rs, plane, plane_to)
     rs[plane] = half[plane]
+    for d in (1, 2, 3):
+        copy(block(me_q), block(me_q), y_s.at[d - 1], y_r.at[d - 1], y_to[d]).start()
+    x_send(me_t, 0)
 
     mask = jnp.where(iota((8, 128), 1) // 16 == iota((8, 128), 0), 1.0 / 16, 0.0)
 
@@ -362,7 +362,7 @@
             zs[z] = sum16(rs)
             small(1, [zs.at[z]] * 15, zs, z, z_to)
 
-        @pl.when(s == 5)
+        @pl.when(s == 4)
         def _():
             small_copy(1, zs).wait_recv()
             ag[plane] = sum16(zs)
@@ -379,7 +379,7 @@
             form(near(e), 64 * near(e))
             grad_copy(64 * near(e), e).start()
 
-        @pl.when(s == 6)
+        @pl.when(s == 5)
         def _():
             small_copy(2, ag).wait_recv()
             for k in range(16):
@@ -392,7 +392,9 @@
 
         pl.when(s == STOPS)(land)
 
-        @pl.loop(jnp.where(s == 8, 8, 0), jnp.where(s <= 6, 0, 8 * (s - 6)))
+        wide = jnp.where((zlo <= 1) | (zlo >= ZLO - 2), 6, 4)
+
+        @pl.loop(jnp.where(s <= 6, 0, wide * (s - 6)), jnp.where(s <= 5, 0, jnp.where(s == 8, 16, wide * (s - 5))))
         def _(j):
             query_batch(j)
 

time: 76.3 us -> 74.1 us (0.971)
  Pallas kernels: 74.9 us -> 72.6 us
    pallas_call x1, Pallas kernels: 74.9 us -> 72.6 us  [body(): pl.pallas_call(functools.partial(kernel, tokens), out_shape=jax.ShapeDtyp...]
where the time goes in v6:
time: 74.1 us; the launch traced here: 73.9 us
  Pallas kernels  72.6 us (98%)
  local copies, waits for them, and re-layouts  1.32 us (2%)
    pallas_call x1, Pallas kernels, body(): pl.pallas_call(functools.partial(kernel, tokens), out_shape=jax.ShapeDtyp...  72.6 us

profile of v6, /device:TPU:1, one launch (start us, length us, event | category | flops | bytes accessed | tf_op | source)
XLA Modules:
  0.0 73.9 jit_solution(1950211862504607349)
XLA Ops:
  0.0 72.6 %influence.1 = f32[1024,512]{1,0:T(8,128)S(1)} custom-call(bf16[1024,128]{1,0:T(8,128)(2,1)} %bitcast.2, bf16[256,128]{1,0:T(8,128)(2,1)} %bitcast.3), custom_call_target="tpu_custom_call" | custom-call | tf_op jit(solution)/shard_map/influence/pallas_call | solution.py:483
  72.6 1.3 %copy.4 = f32[1024,512]{1,0:T(8,128)} copy(f32[1024,512]{1,0:T(8,128)S(1)} %influence.1) | data formatting | bytes 4194304
